TPU v7x, 32 devices: a whole 2x2x4 slice. The times are simulated.
32 devices in a mesh: src: 8 (over z, x), row: 4 (over y, core).
Axes of the slice: x: 2, y: 2, z: 4, core: 2. Of those that a mesh axis runs over, the one named last changes fastest.
Arguments:
- right_side: float32 [2, 8192, 2048], P(None, 'row', 'src'), may hold values from -6 to 6
- pivot_inverse: float32 [2, 2, 512, 512], P(None, None, 'src')
- ancestor_panel: float32 [2, 2, 4096, 512], P(None, None, ('row', 'src')), may hold values from -0.1875 to 0.1875
- ancestors: int32 [2, 4096], P(None, 'row'), may hold values from -1 to 2047, as said below
- pivot_block: int32 [2], replicated, may hold values from 0 to 15, as said below
Outputs:
- forward: float32 [2, 8192, 2048], P(None, 'row', 'src')
Inputs may be any that keep to these rules, and one draw needn't show every extreme that they name: pivot_block holds 2 distinct blocks of 512 rows; one of them is always the last block. `ancestors`: for supernode k and row device r, slots r * 1024 to r * 1024 + 1023 hold distinct rising local rows of that device followed by -1 in the remaining slots; they never touch the pivot rows of supernodes 0 to k, and for k below 1 they include every pivot row of supernode k + 1 that lies on that device; for each supernode some row device fills all 1024 slots.
All inputs are finite; a program needn't handle non-finite values.
Results may differ from a plain program's by a relative error of at most 0.0001.
Values sent between devices are 32-bit elements; how exact they have to be, the bound alone decides.
A program may use at most 128 MiB of HBM per device.

v0:
```python
import functools

import jax
import jax.numpy as jnp
from jax import lax
from jax.experimental import pallas as pl
from jax.experimental.pallas import tpu as pltpu
from jax.sharding import PartitionSpec as P

MESH = pl.DeviceIdType.MESH
F32, BF16 = jnp.float32, jnp.bfloat16
TILE = 256


def halves(value):
    high = value.astype(BF16)
    return high, (value - high.astype(F32)).astype(BF16)


def mm(a, b):
    return jnp.dot(a, b, preferred_element_type=F32)


def mm3(a, b_high, b_low):
    high, low = halves(a)
    return mm(high, b_high) + (mm(high, b_low) + mm(low, b_high))


def kernel(n_src, n_row, front_ref, inverse_ref, panel_ref, slots_ref, block_ref, out_ref,
           pan, inv, cand, core_in, chip_sum, row_in, sol, w_high, w_low, u_high, u_low,
           local_sem, hop_send, hop_recv, inv_send, inv_recv, piv_send, piv_recv):
    nodes, _, shard, depth = panel_ref.shape
    inv_rows = inverse_ref.shape[2]
    quarter = depth // n_row
    half = front_ref.shape[2] // 2
    per_device = front_ref.shape[1] // depth
    slots = slots_ref.shape[1]
    nz, ny = n_src // 2, n_row // 2

    src, row = lax.axis_index("src"), lax.axis_index("row")
    z, x = src // 2, src % 2
    y, core = row // 2, row % 2
    up = {"src": src + 2, "row": row}
    down = {"src": src - 2, "row": row}
    across = {"src": z * 2 + (1 - x), "row": row}
    mate = {"src": src, "row": y * 2 + (1 - core)}
    far = [{"src": src, "row": (y + d) % ny * 2 + core} for d in range(1, ny)]

    def place(unit, index):
        if unit == 0:
            rows = pl.ds(pl.multiple_of(index * inv_rows, 8), inv_rows)
            return inv.at[:, :, row, rows, :]
        rows = pl.ds(pl.multiple_of(index * shard, 8), shard)
        return pan.at[unit - 1, :, rows, :]

    own = [pltpu.make_async_copy(
        inverse_ref.at[:, :, :, pl.ds(pl.multiple_of(row * quarter, 128), quarter)],
        place(0, src), local_sem.at[0])]
    own += [pltpu.make_async_copy(panel_ref.at[k], place(k + 1, src), local_sem.at[k + 1])
            for k in range(nodes)]
    for copy in own:
        copy.start()

    barrier = pltpu.get_barrier_semaphore()

    def greet(device):
        pl.semaphore_signal(barrier, inc=1, device_id=device, device_id_type=MESH)

    @pl.when(z + 1 < nz)
    def _():
        greet(up)

    @pl.when(z > 0)
    def _():
        greet(down)

    for device in [across, mate] + far:
        greet(device)

    ends = jnp.where(z + 1 < nz, 1, 0) + jnp.where(z > 0, 1, 0)
    pl.semaphore_wait(barrier, 2 + len(far) + ends)

    def hop(unit, jz, jx, way, device):
        index = jz * 2 + jx
        ref = place(unit, index)
        return pltpu.make_async_remote_copy(
            src_ref=ref, dst_ref=ref, send_sem=hop_send.at[unit, way, jz],
            recv_sem=hop_recv.at[unit, index], device_id=device, device_id_type=MESH)

    def go_up(unit, jz):
        @pl.when(z + 1 < nz)
        def _():
            hop(unit, jz, x, 0, up).start()

    def go_down(unit, jz):
        @pl.when(z > 0)
        def _():
            hop(unit, jz, x, 1, down).start()

    def go_across(unit, jz):
        hop(unit, jz, x, 2, across).start()

    def own_sends(unit):
        own[unit].wait()
        go_up(unit, z)
        go_down(unit, z)
        go_across(unit, z)

    def step(unit, t):
        below, above = z - t, z + t

        @pl.when(below >= 0)
        def _():
            hop(unit, below, x, 2, across).wait_recv()
            go_up(unit, below)
            go_across(unit, below)

        @pl.when(above < nz)
        def _():
            hop(unit, above, x, 2, across).wait_recv()
            go_down(unit, above)
            go_across(unit, above)

    def steps(unit, first, last):
        @pl.loop(first, last)
        def _(t):
            step(unit, t)

    def across_wait(unit):
        @pl.loop(0, nz)
        def _(j):
            hop(unit, j, 1 - x, 2, across).wait_recv()

    def sends_wait(unit):
        @pl.loop(0, nz)
        def _(j):
            @pl.when((j <= z) & (z + 1 < nz))
            def _():
                hop(unit, j, x, 0, up).wait_send()

            @pl.when((j >= z) & (z > 0))
            def _():
                hop(unit, j, x, 1, down).wait_send()

            hop(unit, j, x, 2, across).wait_send()

    def inv_copy(node, owner_y, owner_core, way, device):
        owner = owner_y * 2 + owner_core
        ref = inv.at[node, :, owner]
        return pltpu.make_async_remote_copy(
            src_ref=ref, dst_ref=ref, send_sem=inv_send.at[node, way],
            recv_sem=inv_recv.at[node, owner], device_id=device, device_id_type=MESH)

    def inv_start(node):
        for d, device in enumerate(far):
            inv_copy(node, y, core, ny + d, device).start()
        inv_copy(node, y, core, 0, mate).start()

    def inv_relay(node):
        for d in range(1, ny):
            other = (y + d) % ny
            inv_copy(node, other, core, 0, mate).wait_recv()
            inv_copy(node, other, core, d, mate).start()

    def inv_finish(node):
        for d in range(ny):
            inv_copy(node, (y + d) % ny, 1 - core, 0, mate).wait_recv()

    def inv_sends_wait(node):
        for d, device in enumerate(far):
            inv_copy(node, y, core, ny + d, device).wait_send()
        for d in range(ny):
            inv_copy(node, (y + d) % ny, core, d, mate).wait_send()

    def copy_of(node, way, source, target, device):
        return pltpu.make_async_remote_copy(
            src_ref=source, dst_ref=target, send_sem=piv_send.at[node, way],
            recv_sem=piv_recv.at[node, way], device_id=device, device_id_type=MESH)

    def core_copy(node):
        return copy_of(node, 0, cand.at[node, 1 - core], core_in.at[node], mate)

    def chip_copy(node, d):
        return copy_of(node, 2 + d, chip_sum.at[node], row_in.at[node, d], far[d])

    def sol_copy(node, which):
        return copy_of(node, 1, sol.at[node, which], sol.at[node, which], mate)

    def offer(node, front):
        for c in range(2):
            for h in range(2):
                total = jnp.zeros((depth, half), F32)
                for b in range(per_device):
                    mine = block_ref[node] == row * per_device + b
                    total = jnp.where(
                        mine, front[c, b * depth:(b + 1) * depth, h * half:(h + 1) * half], total)
                cand[node, h, c] = total
        core_copy(node).start()

    def offer_chip(node):
        core_copy(node).wait_recv()
        chip_sum[node] = cand[node, core] + core_in[node]
        for d in range(ny - 1):
            chip_copy(node, d).start()

    def solve(node):
        for d in range(ny - 1):
            chip_copy(node, d).wait_recv()
        pivot = [chip_sum[node, c] for c in range(2)]
        for d in range(ny - 1):
            pivot = [pivot[c] + row_in[node, d, c] for c in range(2)]
        b_high, b_low = halves(jnp.concatenate(pivot, axis=1))
        for first in range(0, depth, TILE):
            rows = slice(first, first + TILE)
            real, imag = [
                mm3(jnp.concatenate([inv[node, c, q, rows, :] for q in range(n_row)], axis=1),
                    b_high, b_low) for c in range(2)]
            sol[node, core, 0, rows, :] = real[:, :half] - imag[:, half:]
            sol[node, core, 1, rows, :] = real[:, half:] + imag[:, :half]
        sol_copy(node, core).start()
        sol_copy(node, 1 - core).wait_recv()
        for c in range(2):
            for h in range(2):
                high, low = halves(sol[node, h, c])
                lanes = slice(c * 2 * half + h * half, c * 2 * half + (h + 1) * half)
                other = slice((1 - c) * 2 * half + h * half, (1 - c) * 2 * half + (h + 1) * half)
                w_high[:depth, lanes] = high
                w_low[:depth, lanes] = low
                w_high[depth:, other] = -high if c == 1 else high
                w_low[depth:, other] = -low if c == 1 else low

    def project(node, first, last):
        @pl.loop(first, last)
        def _(i):
            rows = pl.ds(pl.multiple_of(i * TILE, TILE), TILE)
            factor = jnp.concatenate([pan[node, 0, rows, :], pan[node, 1, rows, :]], axis=1)
            high, low = halves(mm3(factor, w_high[...], w_low[...]))
            u_high[rows, :] = high
            u_low[rows, :] = low

    def apply(node, front):
        @pl.loop(0, front_ref.shape[1] // TILE)
        def _(i):
            start = pl.multiple_of(i * TILE, TILE)
            rows = pl.ds(start, TILE)
            places = start + lax.broadcasted_iota(jnp.int32, (TILE, slots), 0)
            chosen = jnp.where(places == slots_ref[node:node + 1, :], 1.0, 0.0).astype(BF16)
            change = mm(chosen, u_high[...]) + mm(chosen, u_low[...])
            mine = block_ref[node] == row * per_device + start // depth
            inner = pl.ds(pl.multiple_of(start % depth, TILE), TILE)
            for c in range(2):
                for h in range(2):
                    lanes = slice(h * half, (h + 1) * half)
                    base = jnp.where(mine, sol[node, h, c, inner, :], front[c, rows, lanes])
                    first = c * 2 * half + h * half
                    out_ref[c, rows, lanes] = base - change[:, first:first + half]

    own_sends(0)
    own_sends(1)
    offer(0, front_ref)
    steps(0, 1, nz)
    across_wait(0)
    inv_start(0)
    offer_chip(0)
    steps(1, 1, nz)
    for node in range(nodes):
        front = front_ref if node == 0 else out_ref
        inv_relay(node)
        inv_finish(node)
        if node + 1 < nodes:
            own_sends(node + 2)
            inv_start(node + 1)
        solve(node)
        across_wait(node + 1)
        project(node, 0, slots // TILE)
        apply(node, front)
        if node + 1 < nodes:
            offer(node + 1, out_ref)
            steps(node + 2, 1, 2)
            offer_chip(node + 1)
            steps(node + 2, 2, nz)

    for unit in range(nodes + 1):
        sends_wait(unit)
    for node in range(nodes):
        inv_sends_wait(node)
        core_copy(node).wait_send()
        sol_copy(node, core).wait_send()
        for d in range(ny - 1):
            chip_copy(node, d).wait_send()


def solution(mesh):
    n_src, n_row = mesh.shape["src"], mesh.shape["row"]

    def local(right_side, pivot_inverse, ancestor_panel, ancestors, pivot_block):
        nodes, _, shard, depth = ancestor_panel.shape
        slots = shard * n_src
        inv_rows = pivot_inverse.shape[2] * n_src
        columns = right_side.shape[2]
        half, quarter = columns // 2, depth // n_row
        nz, ny = n_src // 2, n_row // 2
        dma = pltpu.SemaphoreType.DMA
        vmem = pl.BlockSpec(memory_space=pltpu.VMEM)
        anywhere = pl.BlockSpec(memory_space=pl.ANY)
        return pl.pallas_call(
            functools.partial(kernel, n_src, n_row),
            out_shape=jax.ShapeDtypeStruct(right_side.shape, F32),
            in_specs=[vmem, anywhere, anywhere, vmem, pl.BlockSpec(memory_space=pltpu.SMEM)],
            out_specs=vmem,
            scratch_shapes=[
                pltpu.VMEM((nodes, 2, slots, depth), F32),
                pltpu.VMEM((nodes, 2, n_row, inv_rows, quarter), F32),
                pltpu.VMEM((nodes, 2, 2, depth, half), F32),
                pltpu.VMEM((nodes, 2, depth, half), F32),
                pltpu.VMEM((nodes, 2, depth, half), F32),
                pltpu.VMEM((nodes, ny - 1, 2, depth, half), F32),
                pltpu.VMEM((nodes, 2, 2, depth, half), F32),
                pltpu.VMEM((2 * depth, 2 * columns), BF16),
                pltpu.VMEM((2 * depth, 2 * columns), BF16),
                pltpu.VMEM((slots, 2 * columns), BF16),
                pltpu.VMEM((slots, 2 * columns), BF16),
                dma((nodes + 1,)),
                dma((nodes + 1, 3, nz)),
                dma((nodes + 1, n_src)),
                dma((nodes, 2 * ny)),
                dma((nodes, n_row)),
                dma((nodes, ny + 1)),
                dma((nodes, ny + 1)),
            ],
            compiler_params=pltpu.CompilerParams(
                collective_id=0, has_side_effects=True, vmem_limit_bytes=56 * 1024 * 1024),
        )(right_side, pivot_inverse, ancestor_panel, ancestors, pivot_block)

    in_specs = (
        P(None, "row", "src"),
        P(None, None, "src", None),
        P(None, None, ("row", "src"), None),
        P(None, "row"),
        P(),
    )
    out_specs = P(None, "row", "src")
    return jax.shard_map(local, mesh=mesh, in_specs=in_specs, out_specs=out_specs, check_vma=False)
```

profile of v0, /device:TPU:0, one launch (start us, length us, event | category | flops | bytes accessed | tf_op | source)
XLA Modules:
  0.0 128.8 jit_solution(14860740285151368206)
XLA Ops:
  0.0 124.3 %shard_map.55 = f32[2,2048,256]{2,1,0:T(8,128)} custom-call(f32[2,2048,256]{2,1,0:T(8,128)} %front_ref.1, f32[2,2,64,512]{3,2,1,0:T(8,128)} %inverse_ref.1, f32[2,2,128,512]{3,2,1,0:T(8,128)} %panel_ref.1, s32[2,1024]{1,0:T(2,128)} %slots_ref.1, s32[2]{0:T(128)} %block_ref.1), custom_call_target="tpu_custom_call" | custom-call | tf_op jit(solution)/shard_map/pallas_call | solution.py:306
  124.3 4.5 %copy.7 = f32[2,2048,256]{2,1,0:T(8,128)} copy(f32[2,2048,256]{2,1,0:T(8,128)} %shard_map.55) | data formatting | bytes 8388608
where the time goes:
time: 129 us
  Pallas kernels  124 us (96%)
  local copies, waits for them, and re-layouts  4.47 us (3%)
    pallas_call x1, Pallas kernels, local(): pl.pallas_call(functools.partial(kernel, n_src, n_row), out_shape=jax.Sha...  124 us
    unnamed x1, local copies, waits for them, and re-layouts  4.47 us

commit v1 on v0

--- a/solution.py
+++ b/solution.py
@@ -46,17 +46,16 @@
     mate = {"src": src, "row": y * 2 + (1 - core)}
     far = [{"src": src, "row": (y + d) % ny * 2 + core} for d in range(1, ny)]
 
-    def place(unit, index):
+    def place(unit, jz, jx, part=slice(None)):
         if unit == 0:
-            rows = pl.ds(pl.multiple_of(index * inv_rows, 8), inv_rows)
-            return inv.at[:, :, row, rows, :]
-        rows = pl.ds(pl.multiple_of(index * shard, 8), shard)
-        return pan.at[unit - 1, :, rows, :]
+            rows = pl.ds(pl.multiple_of((jz * 2 + jx) * inv_rows, 8), inv_rows)
+            return inv.at[:, part, row, rows, :]
+        return pan.at[unit - 1, part, jx, pl.ds(pl.multiple_of(jz * shard, 8), shard), :]
 
     own = [pltpu.make_async_copy(
         inverse_ref.at[:, :, :, pl.ds(pl.multiple_of(row * quarter, 128), quarter)],
-        place(0, src), local_sem.at[0])]
-    own += [pltpu.make_async_copy(panel_ref.at[k], place(k + 1, src), local_sem.at[k + 1])
+        place(0, z, x), local_sem.at[0])]
+    own += [pltpu.make_async_copy(panel_ref.at[k], place(k + 1, z, x), local_sem.at[k + 1])
             for k in range(nodes)]
     for copy in own:
         copy.start()
@@ -80,12 +79,20 @@
     ends = jnp.where(z + 1 < nz, 1, 0) + jnp.where(z > 0, 1, 0)
     pl.semaphore_wait(barrier, 2 + len(far) + ends)
 
-    def hop(unit, jz, jx, way, device):
-        index = jz * 2 + jx
-        ref = place(unit, index)
+    pair = z + 1 - 2 * (z % 2)
+    pair_device = {"src": pair * 2 + x, "row": row}
+
+    def hop(unit, jz, jx, way, device, part=slice(None)):
+        ref = place(unit, jz, jx, part)
         return pltpu.make_async_remote_copy(
             src_ref=ref, dst_ref=ref, send_sem=hop_send.at[unit, way, jz],
-            recv_sem=hop_recv.at[unit, index], device_id=device, device_id_type=MESH)
+            recv_sem=hop_recv.at[unit, jz * 2 + jx], device_id=device, device_id_type=MESH)
+
+    def extra_hop(unit, jz):
+        ref = place(unit, jz, 1 - x, 1)
+        return pltpu.make_async_remote_copy(
+            src_ref=ref, dst_ref=ref, send_sem=hop_send.at[unit, 3, 0],
+            recv_sem=hop_recv.at[unit, n_src], device_id=pair_device, device_id_type=MESH)
 
     def go_up(unit, jz):
         @pl.when(z + 1 < nz)
@@ -98,7 +105,17 @@
             hop(unit, jz, x, 1, down).start()
 
     def go_across(unit, jz):
-        hop(unit, jz, x, 2, across).start()
+        @pl.when(jz == pair)
+        def _():
+            hop(unit, jz, x, 2, across, 0).start()
+
+        @pl.when(jz != pair)
+        def _():
+            hop(unit, jz, x, 2, across).start()
+
+    def extra(unit):
+        hop(unit, z, 1 - x, 2, across).wait_recv()
+        extra_hop(unit, z).start()
 
     def own_sends(unit):
         own[unit].wait()
@@ -129,7 +146,12 @@
     def across_wait(unit):
         @pl.loop(0, nz)
         def _(j):
-            hop(unit, j, 1 - x, 2, across).wait_recv()
+            @pl.when((j != z) & (j != pair))
+            def _():
+                hop(unit, j, 1 - x, 2, across).wait_recv()
+
+        hop(unit, pair, 1 - x, 2, across, 0).wait_recv()
+        extra_hop(unit, pair).wait_recv()
 
     def sends_wait(unit):
         @pl.loop(0, nz)
@@ -142,7 +164,12 @@
             def _():
                 hop(unit, j, x, 1, down).wait_send()
 
-            hop(unit, j, x, 2, across).wait_send()
+            @pl.when(j != pair)
+            def _():
+                hop(unit, j, x, 2, across).wait_send()
+
+        hop(unit, pair, x, 2, across, 0).wait_send()
+        extra_hop(unit, z).wait_send()
 
     def inv_copy(node, owner_y, owner_core, way, device):
         owner = owner_y * 2 + owner_core
@@ -229,14 +256,17 @@
                 w_high[depth:, other] = -high if c == 1 else high
                 w_low[depth:, other] = -low if c == 1 else low
 
-    def project(node, first, last):
-        @pl.loop(first, last)
+    def project(node, column):
+        @pl.loop(0, slots // 2 // TILE)
         def _(i):
             rows = pl.ds(pl.multiple_of(i * TILE, TILE), TILE)
-            factor = jnp.concatenate([pan[node, 0, rows, :], pan[node, 1, rows, :]], axis=1)
+            factor = jnp.concatenate([pan[node, c, column, rows, :] for c in range(2)], axis=1)
             high, low = halves(mm3(factor, w_high[...], w_low[...]))
-            u_high[rows, :] = high
-            u_low[rows, :] = low
+            for g in range(TILE // shard):
+                first = ((i * (TILE // shard) + g) * 2 + column) * shard
+                target = pl.ds(pl.multiple_of(first, 16), shard)
+                u_high[target, :] = high[g * shard:(g + 1) * shard]
+                u_low[target, :] = low[g * shard:(g + 1) * shard]
 
     def apply(node, front):
         @pl.loop(0, front_ref.shape[1] // TILE)
@@ -259,26 +289,33 @@
     own_sends(1)
     offer(0, front_ref)
     steps(0, 1, nz)
+    extra(0)
     across_wait(0)
     inv_start(0)
     offer_chip(0)
     steps(1, 1, nz)
+    extra(1)
+    inv_relay(0)
     for node in range(nodes):
         front = front_ref if node == 0 else out_ref
-        inv_relay(node)
+        more = node + 1 < nodes
         inv_finish(node)
-        if node + 1 < nodes:
+        if more:
             own_sends(node + 2)
             inv_start(node + 1)
         solve(node)
+        project(node, x)
         across_wait(node + 1)
-        project(node, 0, slots // TILE)
+        if more:
+            steps(node + 2, 1, 2)
+        project(node, 1 - x)
         apply(node, front)
-        if node + 1 < nodes:
+        if more:
             offer(node + 1, out_ref)
-            steps(node + 2, 1, 2)
+            inv_relay(node + 1)
             offer_chip(node + 1)
             steps(node + 2, 2, nz)
+            extra(node + 2)
 
     for unit in range(nodes + 1):
         sends_wait(unit)
@@ -309,7 +346,7 @@
             in_specs=[vmem, anywhere, anywhere, vmem, pl.BlockSpec(memory_space=pltpu.SMEM)],
             out_specs=vmem,
             scratch_shapes=[
-                pltpu.VMEM((nodes, 2, slots, depth), F32),
+                pltpu.VMEM((nodes, 2, 2, slots // 2, depth), F32),
                 pltpu.VMEM((nodes, 2, n_row, inv_rows, quarter), F32),
                 pltpu.VMEM((nodes, 2, 2, depth, half), F32),
                 pltpu.VMEM((nodes, 2, depth, half), F32),
@@ -321,8 +358,8 @@
                 pltpu.VMEM((slots, 2 * columns), BF16),
                 pltpu.VMEM((slots, 2 * columns), BF16),
                 dma((nodes + 1,)),
-                dma((nodes + 1, 3, nz)),
-                dma((nodes + 1, n_src)),
+                dma((nodes + 1, 4, nz)),
+                dma((nodes + 1, n_src + 1)),
                 dma((nodes, 2 * ny)),
                 dma((nodes, n_row)),
                 dma((nodes, ny + 1)),

time: 129 us -> 123 us (0.953)
  Pallas kernels: 124 us -> 118 us
    pallas_call x1, Pallas kernels: 124 us -> 118 us  [local(): pl.pallas_call(functools.partial(kernel, n_src, n_row), out_shape=jax.Sha...]
where the time goes in v1:
time: 123 us
  Pallas kernels  118 us (96%)
  local copies, waits for them, and re-layouts  4.47 us (4%)
    pallas_call x1, Pallas kernels, local(): pl.pallas_call(functools.partial(kernel, n_src, n_row), out_shape=jax.Sha...  118 us
    unnamed x1, local copies, waits for them, and re-layouts  4.47 us

profile of v1, /device:TPU:0, one launch (start us, length us, event | category | flops | bytes accessed | tf_op | source)
XLA Modules:
  0.0 122.9 jit_solution(4858916601535548989)
XLA Ops:
  0.0 118.4 %shard_map.55 = f32[2,2048,256]{2,1,0:T(8,128)} custom-call(f32[2,2048,256]{2,1,0:T(8,128)} %front_ref.1, f32[2,2,64,512]{3,2,1,0:T(8,128)} %inverse_ref.1, f32[2,2,128,512]{3,2,1,0:T(8,128)} %panel_ref.1, s32[2,1024]{1,0:T(2,128)} %slots_ref.1, s32[2]{0:T(128)} %block_ref.1), custom_call_target="tpu_custom_call" | custom-call | tf_op jit(solution)/shard_map/pallas_call | solution.py:343
  118.4 4.5 %copy.7 = f32[2,2048,256]{2,1,0:T(8,128)} copy(f32[2,2048,256]{2,1,0:T(8,128)} %shard_map.55) | data formatting | bytes 8388608
